TPU v7x, 32 devices: a whole 2x2x4 slice. The times are simulated.
32 devices in a mesh: ctx: 16 (over z, y, core), tp: 2 (over x).
Axes of the slice: x: 2, y: 2, z: 4, core: 2. Of those that a mesh axis runs over, the one named last changes fastest.
Arguments:
- attended: bfloat16 [4096, 4096], P('ctx', 'tp'), may hold values from -6 to 6
- out_proj: bfloat16 [4096, 4096], P('tp'), may hold values from -0.09375 to 0.09375
- residual: bfloat16 [4096, 4096], P(('ctx', 'tp')), may hold values from -6 to 6
- norm_gain: float32 [4096], replicated, may hold values from 0.5 to 1.5
- cond_proj: bfloat16 [4096, 2048], P(None, 'tp'), may hold values from -0.09375 to 0.09375
- noise_proj: bfloat16 [128, 2048], P(None, 'tp'), may hold values from -0.5 to 0.5
- latent_proj: bfloat16 [2048, 128], P('tp'), may hold values from -0.176776695 to 0.176776695
- noise_draws: bfloat16 [4096, 8, 128], P('ctx'), may hold values from -6 to 6
- targets: bfloat16 [4096, 128], P(('ctx', 'tp')), may hold values from -9 to 9
Outputs:
- energies: float32 [4096], P(('ctx', 'tp'))
- cond_grad: bfloat16 [4096, 2048], P(None, 'tp')
- noise_grad: bfloat16 [128, 2048], P(None, 'tp')
- latent_grad: bfloat16 [2048, 128], P('tp')
All inputs are finite; a program needn't handle non-finite values.
Results may differ from a plain program's by a relative error of at most 0.018.
Values may be sent and summed in bfloat16 or wider, within the bound.
A program may use at most 128 MiB of HBM per device.

v0:
```python
import jax
import jax.numpy as jnp
from jax import lax
from jax.sharding import PartitionSpec as P

D = 4096
HW = 2048
LAT = 128
NZ = 128


def silu_slope(values):
    sigmoid = jax.nn.sigmoid(values)
    return sigmoid * (1.0 + values * (1.0 - sigmoid))


def energy_score(samples, goal_rows):
    n_draws = samples.shape[1]
    diff_t = samples - goal_rows[:, None, :]
    dist_t = jnp.sqrt(jnp.sum(diff_t * diff_t, axis=-1) + 1.0)
    diff_p = samples[:, :, None, :] - samples[:, None, :, :]
    dist_p = jnp.sqrt(jnp.sum(diff_p * diff_p, axis=-1) + 1.0)
    off_diag = 1.0 - jnp.eye(n_draws, dtype=jnp.float32)
    pair_count = n_draws * (n_draws - 1)
    energies = jnp.mean(dist_t, axis=1) - jnp.sum(dist_p * off_diag, axis=(1, 2)) / (
        2.0 * pair_count
    )
    slopes = (
        diff_t / (n_draws * dist_t[..., None])
        - jnp.sum(diff_p / dist_p[..., None], axis=2) / pair_count
    )
    return (energies, slopes.astype(jnp.bfloat16))


def row_contract(left, right):
    return lax.dot_general(
        left, right, (((0,), (0,)), ((), ())), preferred_element_type=jnp.float32
    )


def square_sum(cond_part, noise_part, latent_part):
    return (
        jnp.sum(cond_part * cond_part)
        + jnp.sum(noise_part * noise_part)
        + jnp.sum(latent_part * latent_part)
    )


def on_device(
    attended,
    out_proj,
    residual,
    norm_gain,
    cond_proj,
    noise_proj,
    latent_proj,
    noise_draws,
    targets,
):
    summed = lax.psum_scatter(
        jnp.dot(attended, out_proj, preferred_element_type=jnp.float32).astype(jnp.bfloat16),
        "tp",
        scatter_dimension=0,
        tiled=True,
    ).astype(jnp.float32)
    hidden = residual.astype(jnp.float32) + summed
    normed = (
        hidden * lax.rsqrt(jnp.mean(hidden * hidden, axis=-1, keepdims=True) + 1e-05) * norm_gain
    ).astype(jnp.bfloat16)
    gathered = lax.all_gather(normed, "tp", axis=0, tiled=True)
    condition = jnp.dot(gathered, cond_proj, preferred_element_type=jnp.float32)
    preact = condition[:, None, :] + jnp.einsum(
        "rsn,nh->rsh", noise_draws, noise_proj, preferred_element_type=jnp.float32
    )
    activation = jax.nn.silu(preact).astype(jnp.bfloat16)
    partial_samples = jnp.einsum(
        "rsh,hl->rsl", activation, latent_proj, preferred_element_type=jnp.float32
    )
    own_samples = lax.psum_scatter(partial_samples, "tp", scatter_dimension=0, tiled=True)
    energies, own_slopes = energy_score(own_samples, targets.astype(jnp.float32))
    slopes = lax.all_gather(own_slopes, "tp", axis=0, tiled=True)
    latent_part = jnp.einsum("rsh,rsl->hl", activation, slopes, preferred_element_type=jnp.float32)
    backward = jnp.einsum("rsl,hl->rsh", slopes, latent_proj, preferred_element_type=jnp.float32)
    pre_grad = (backward * silu_slope(preact)).astype(jnp.bfloat16)
    noise_part = jnp.einsum(
        "rsn,rsh->nh", noise_draws, pre_grad, preferred_element_type=jnp.float32
    )
    cond_slope = jnp.sum(pre_grad, axis=1, dtype=jnp.float32).astype(jnp.bfloat16)
    cond_part = row_contract(gathered, cond_slope)
    param_count = D * HW + NZ * HW + HW * LAT
    cond_sum, noise_sum, latent_sum = lax.psum((cond_part, noise_part, latent_part), "ctx")
    squares_total = lax.psum(square_sum(cond_sum, noise_sum, latent_sum), "tp")
    rescale = lax.rsqrt(squares_total / param_count + 1e-06)
    cond_out = (cond_sum * rescale).astype(jnp.bfloat16)
    noise_out = (noise_sum * rescale).astype(jnp.bfloat16)
    latent_out = (latent_sum * rescale).astype(jnp.bfloat16)
    return (energies, cond_out, noise_out, latent_out)


def solution(mesh):
    return jax.shard_map(
        on_device,
        mesh=mesh,
        in_specs=(
            P("ctx", "tp"),
            P("tp", None),
            P(("ctx", "tp"), None),
            P(),
            P(None, "tp"),
            P(None, "tp"),
            P("tp", None),
            P("ctx", None, None),
            P(("ctx", "tp"), None),
        ),
        out_specs=(P(("ctx", "tp")), P(None, "tp"), P(None, "tp"), P("tp", None)),
        check_vma=False,
    )
```

profile of v0, /device:TPU:0, one launch (start us, length us, event | category | flops | bytes accessed | tf_op | source)
XLA Modules:
  0.0 518.3 jit_solution(2451178643178801793)
XLA Ops:
  8.4 11.4 %convolution_convert_fusion = bf16[256,4096]{1,0:T(8,128)(2,1)} fusion(bf16[256,2048]{1,0:T(8,128)(2,1)S(1)} %copy-done, bf16[2048,4096]{1,0:T(8,128)(2,1)} %param.10), kind=kOutput, calls=%fused_computation.7 | convolution fusion | flops 4296015872 | bytes 19922944 | tf_op jit(solution)/shard_map/dot_general | solution.py:61
  19.9 34.6 %reduce-scatter.3.cloned.1.call-done = bf16[128,4096]{1,0:T(8,128)(2,1)} async-done(((bf16[256,4096]{1,0:T(8,128)(2,1)}), bf16[128,4096]{1,0:T(8,128)(2,1)}) %reduce-scatter.3.cloned.1.call-update) | async-done | bytes 1048592 | tf_op jit(solution)/shard_map/reduce_scatter | solution.py:60
  54.5 1.6 multiply_reduce_fusion.1
  56.2 2.6 multiply_convert_fusion.3
  58.9 33.2 %all-gather.2.cloned.1.call-done = bf16[256,4096]{1,0:T(8,128)(2,1)} async-done(((bf16[128,4096]{1,0:T(8,128)(2,1)}), bf16[256,4096]{1,0:T(8,128)(2,1)}) %all-gather.2.cloned.1.call-update) | async-done | bytes 2097168 | tf_op jit(solution)/shard_map/all_gather | solution.py:70
  92.1 6.3 %fusion.14 = f32[256,1024]{1,0:T(8,128)S(1)} fusion(bf16[256,4096]{1,0:T(8,128)(2,1)} %all-gather.2.cloned.1.call-done, bf16[4096,1024]{1,0:T(8,128)(2,1)} %param.13), kind=kOutput, calls=%fused_computation.40 | convolution fusion | flops 2147483648 | bytes 11534336 | tf_op jit(solution)/shard_map/dot_general | solution.py:71
  98.5 4.7 multiply_convert_fusion.2
  103.2 1.9 copy-done.2
  105.1 2.3 fusion.8
  107.5 20.4 %reduce-scatter.5.cloned.1.call-done = f32[128,8,128]{2,0,1:T(8,128)} async-done(((f32[256,8,128]{2,0,1:T(8,128)}), f32[128,8,128]{2,0,1:T(8,128)}) %reduce-scatter.5.cloned.1.call-update) | async-done | bytes 524304 | tf_op jit(solution)/shard_map/reduce_scatter | solution.py:79
  127.8 1.3 multiply_reduce_fusion.4
  129.2 1.4 copy.30
  132.3 2.0 fusion
  134.5 8.9 %all_gather.7 = bf16[256,8,128]{2,0,1:T(8,128)(2,1)S(1)} all-gather(bf16[128,8,128]{2,0,1:T(8,128)(2,1)S(1)} %fusion.3), channel_id=1, replica_groups=mesh['ctx'=16,'tp'=2] {'tp'}, dimensions={0}, use_global_device_ids=true | all-gather | bytes 786432 | tf_op jit(solution)/shard_map/all_gather | solution.py:81
  143.4 2.1 convolution_bitcast_fusion
  145.5 6.0 %fusion.13 = (bf16[256,1024]{1,0:T(8,128)(2,1)S(1)}, bf16[256,8,1024]{2,0,1:T(8,128)(2,1)S(1)}) fusion(f32[256,8,1024]{2,0,1:T(8,128)} %get-tuple-element.24, f32[256,1024]{1,0:T(8,128)S(1)} %fusion.14, bf16[256,8,128]{2,0,1:T(8,128)(2,1)S(1)} %all_gather.7, bf16[1024,128]{1,0:T(8,128)(2,1)S(1)} %copy-done.9), kind=kOutput, calls=%fused_computation.39 | convolution fusion | flops 559677440 | bytes 14942208 | tf_op jit(solution)/shard_map/rsl,hl->rsh/dot_general | solution.py:83
  151.6 2.1 convolution_bitcast_fusion.1
  153.7 8.1 %fusion.15 = f32[4096,1024]{1,0:T(8,128)} fusion(bf16[256,4096]{1,0:T(8,128)(2,1)S(1)} %copy-done.6, bf16[256,1024]{1,0:T(8,128)(2,1)S(1)} %get-tuple-element.25), kind=kOutput, calls=%fused_computation.41 | convolution fusion | flops 2147483648 | bytes 19398656 | tf_op jit(solution)/shard_map/dot_general | solution.py:36
  161.8 315.6 %all-reduce.3.cloned.1.call-done = (f32[4096,1024]{1,0:T(8,128)}, f32[128,1024]{0,1:T(8,128)}, f32[1024,128]{1,0:T(8,128)}) async-done(((f32[4096,1024]{1,0:T(8,128)}, f32[128,1024]{0,1:T(8,128)}, f32[1024,128]{1,0:T(8,128)}), (f32[4096,1024]{1,0:T(8,128)}, f32[128,1024]{0,1:T(8,128)}, f32[1024,128]{1,0:T(8,128)})) %all-reduce.3.cloned.1.call-update) | async-done | bytes 17825808 | tf_op jit(solution)/shard_map/psum | solution.py:91
  477.4 1.8 multiply_reduce_fusion.2
  479.2 1.8 multiply_reduce_fusion.3
  481.0 10.7 %multiply_reduce_fusion = f32[]{:T(128)} fusion(f32[4096,1024]{1,0:T(8,128)} %get-tuple-element.16), kind=kLoop, calls=%fused_computation.1 | loop fusion | flops 8388607 | bytes 16777220 | tf_op jit(solution)/shard_map/reduce_sum | solution.py:43
  494.1 5.4 %psum.31 = f32[]{:T(128)} all-reduce(f32[]{:T(128)S(6)} %add.83), channel_id=1, replica_groups=mesh['ctx'=16,'tp'=2] {'tp'}, use_global_device_ids=true, to_apply=%region_15.16 | all-reduce | flops 1 | bytes 8 | tf_op jit(solution)/shard_map/psum | solution.py:92
  500.3 9.9 %multiply_convert_fusion = bf16[4096,1024]{1,0:T(8,128)(2,1)} fusion(f32[4096,1024]{1,0:T(8,128)} %get-tuple-element.16, f32[]{:T(128)S(6)} %rsqrt.12), kind=kLoop, calls=%fused_computation | loop fusion | flops 8388608 | bytes 25165828 | tf_op jit(solution)/shard_map/convert_element_type | solution.py:94
  (48 shorter events, 5.5 us)
Async XLA Ops:
  7.2 1.2 copy-start
  7.2 47.3 %copy-start.5 = (bf16[128,4096]{1,0:T(8,128)(2,1)S(1)}, bf16[128,4096]{1,0:T(8,128)(2,1)}, u32[]{:S(2)}) copy-start(bf16[128,4096]{1,0:T(8,128)(2,1)} %param.11) | copy-start | bytes 3145732
  7.2 47.3 %reduce-scatter.3.cloned.1.call-start = ((), (), s32[]{:S(2)}) async-start(), calls=%async_computation.2 | async-start | bytes 3145728 | tf_op jit(solution)/shard_map/reduce_scatter | solution.py:60
  19.8 36.3 %copy-start.11 = (f32[4096]{0:T(1024)S(1)}, f32[4096]{0:T(1024)}, u32[]{:S(2)}) copy-start(f32[4096]{0:T(1024)} %param.12) | copy-start | bytes 49156
  19.9 72.2 %all-gather.2.cloned.1.call-start = ((), (), s32[]{:S(2)}) async-start(), calls=%async_computation.3 | async-start | bytes 3145728 | tf_op jit(solution)/shard_map/all_gather | solution.py:70
  58.8 39.6 %copy-start.12 = (bf16[256,8,128]{2,1,0:T(8,128)(2,1)S(1)}, bf16[256,8,128]{2,1,0:T(8,128)(2,1)}, u32[]{:S(2)}) copy-start(bf16[256,8,128]{2,1,0:T(8,128)(2,1)} %param.16) | copy-start | bytes 1572868
  58.8 39.6 %copy-start.13 = (bf16[128,1024]{1,0:T(8,128)(2,1)S(1)}, bf16[128,1024]{1,0:T(8,128)(2,1)}, u32[]{:S(2)}) copy-start(bf16[128,1024]{1,0:T(8,128)(2,1)} %param.14) | copy-start | bytes 786436
  58.8 69.0 %reduce-scatter.5.cloned.1.call-start = ((), (), s32[]{:S(2)}) async-start(), calls=%async_computation.4 | async-start | bytes 1572864 | tf_op jit(solution)/shard_map/reduce_scatter | solution.py:79
  98.5 6.6 %copy-start.9 = (bf16[1024,128]{1,0:T(8,128)(2,1)S(1)}, bf16[1024,128]{1,0:T(8,128)(2,1)}, u32[]{:S(2)}) copy-start(bf16[1024,128]{1,0:T(8,128)(2,1)} %param.15) | copy-start | bytes 786436
  103.2 1.9 copy-start.2
  103.2 4.3 copy-start.10
  107.4 370.0 %all-reduce.3.cloned.1.call-start = ((), (), s32[]{:S(2)}) async-start(), calls=%async_computation.5 | async-start | bytes 35651584 | tf_op jit(solution)/shard_map/psum | solution.py:91
  127.8 6.4 %copy-start.4 = (f32[128,8,128]{2,0,1:T(8,128)S(1)}, f32[128,8,128]{2,0,1:T(8,128)}, u32[]{:S(2)}) copy-start(f32[128,8,128]{2,0,1:T(8,128)} %reduce-scatter.5.cloned.1.call-done) | copy-start | bytes 1572868
  132.2 11.2 %copy-start.3 = (bf16[256,8,1024]{2,0,1:T(8,128)(2,1)S(1)}, bf16[256,8,1024]{2,0,1:T(8,128)(2,1)}, u32[]{:S(2)}) copy-start(bf16[256,8,1024]{2,0,1:T(8,128)(2,1)} %copy-done.2) | copy-start | bytes 12582916
  151.6 2.1 copy-start.6
  500.2 9.9 %copy-start.8 = (f32[1024,128]{1,0:T(8,128)S(1)}, f32[1024,128]{1,0:T(8,128)}, u32[]{:S(2)}) copy-start(f32[1024,128]{1,0:T(8,128)} %get-tuple-element.18) | copy-start | bytes 1572868
  500.2 10.6 %copy-start.7 = (f32[128,1024]{0,1:T(8,128)S(1)}, f32[128,1024]{0,1:T(8,128)}, u32[]{:S(2)}) copy-start(f32[128,1024]{0,1:T(8,128)} %get-tuple-element.17) | copy-start | bytes 1572868
  500.2 11.5 %copy-start.1 = (bf16[256,2048]{1,0:T(8,128)(2,1)S(1)}, bf16[256,2048]{1,0:T(8,128)(2,1)}, u32[]{:S(2)}) copy-start(bf16[256,2048]{1,0:T(8,128)(2,1)} %param.9) | copy-start | bytes 3145732
Sparse Core Ops, SparseCore 0:
  20.0 34.4 reduce-scatter.2
  58.9 33.1 all-gather.1
  107.5 20.3 reduce-scatter.4
  161.9 315.4 all-reduce.2
where the time goes:
time: 519 us; the launch traced here: 518 us
  waiting for transfers between devices  404 us (78%)
  matrix products  43 us (8%)
  other arithmetic  34.5 us (7%)
  between operations  16.6 us (3%)
  blocking collectives  14.3 us (3%)
  local copies, waits for them, and re-layouts  5.77 us (1%)
    psum x1, waiting for transfers between devices, on_device(): lax.psum((cond_part, noise_part, latent_part), 'ctx')  316 us
    reduce_scatter x1, waiting for transfers between devices, on_device(): lax.psum_scatter(jnp.dot(attended, out_proj, preferred_element_type=jnp.f...  34.6 us
    all_gather x1, waiting for transfers between devices, on_device(): gathered = lax.all_gather(normed, 'tp', axis=0, tiled=True)  33.2 us
    reduce_scatter x1, waiting for transfers between devices, on_device(): lax.psum_scatter(partial_samples, 'tp', scatter_dimension=0, tiled=True)  20.4 us
    dot_general x1, matrix products, on_device(): jnp.dot(attended, out_proj, preferred_element_type=jnp.float32)  11.4 us
    reduce_sum x1, other arithmetic, square_sum(): jnp.sum(cond_part * cond_part) + jnp.sum(noise_part * noise_part)  10.7 us
  transfers between devices with their start and end apart: 4, of which 4 were waited for; matrix products, arithmetic and copies ran while one was open for 0% of the time, Pallas kernels for 0%

commit v1 on v0

--- a/solution.py
+++ b/solution.py
@@ -1,7 +1,16 @@
+import functools
+
 import jax
 import jax.numpy as jnp
 from jax import lax
+from jax.experimental import pallas as pl
+from jax.experimental.pallas import tpu as pltpu
 from jax.sharding import PartitionSpec as P
+
+ROWS = 64
+BLOCK = 256
+QUADS = 4
+MESH = pl.DeviceIdType.MESH
 
 D = 4096
 HW = 2048
@@ -38,15 +47,349 @@
     )
 
 
-def square_sum(cond_part, noise_part, latent_part):
-    return (
-        jnp.sum(cond_part * cond_part)
-        + jnp.sum(noise_part * noise_part)
-        + jnp.sum(latent_part * latent_part)
-    )
+def grad_kernel(
+    n_ctx,
+    n_tp,
+    scale_count,
+    rows_ref,
+    slope_ref,
+    small_ref,
+    out_ref,
+    rescale_ref,
+    slopes,
+    smalls,
+    prod,
+    up,
+    landed,
+    squares,
+    tp_squares,
+    slope_send,
+    slope_recv,
+    small_send,
+    small_recv,
+    up_send,
+    up_recv,
+    down_send,
+    down_recv,
+    side_send,
+    side_recv,
+    core_send,
+    core_recv,
+    tp_send,
+    tp_recv,
+):
+    chunks = prod.shape[0]
+    grad_chunks = chunks - 1
+    line = n_ctx // QUADS
+    width = prod.shape[2]
+    me = lax.axis_index("ctx")
+    tp = lax.axis_index("tp")
+    quad = lax.rem(me, QUADS)
+    place = me // QUADS
+    left = place < line // 2
+    depth = jnp.where(left, place, line - 1 - place)
+    middle = depth == line // 2 - 1
+    inward = jnp.where(left, me + QUADS, me - QUADS)
+    outward = jnp.where(left, me - QUADS, me + QUADS)
+    mates = [None] + [
+        (me - quad) + (quad + m - 2 * ((quad // m) % 2) * m if m < 3 else 3 - quad) for m in (1, 2, 3)
+    ]
+    mate_quads = [quad] + [mates[m] - (me - quad) for m in (1, 2, 3)]
+    core, side = mates[1], mates[2]
+
+    def remote(src, dst, send, recv, target, target_tp=None):
+        return pltpu.make_async_remote_copy(
+            src_ref=src,
+            dst_ref=dst,
+            send_sem=send,
+            recv_sem=recv,
+            device_id=(target, tp if target_tp is None else target_tp),
+            device_id_type=MESH,
+        )
+
+    barrier = pltpu.get_barrier_semaphore()
+    for mate in mates[1:]:
+        pl.semaphore_signal(barrier, inc=1, device_id=(mate, tp), device_id_type=MESH)
+    pl.semaphore_signal(barrier, inc=1, device_id=(inward, tp), device_id_type=MESH)
+
+    @pl.when(depth > 0)
+    def _():
+        pl.semaphore_signal(barrier, inc=1, device_id=(outward, tp), device_id_type=MESH)
+
+    for step in range(1, n_tp):
+        pl.semaphore_signal(
+            barrier, inc=1, device_id=(me, lax.rem(tp + step, n_tp)), device_id_type=MESH
+        )
+    pl.semaphore_wait(barrier, 4 + n_tp - 1 + jnp.where(depth > 0, 1, 0))
+
+    slope_side = remote(slope_ref, slopes.at[1], slope_send.at[1], slope_recv.at[1], side)
+    slope_core = remote(slope_ref, slopes.at[0], slope_send.at[0], slope_recv.at[0], core)
+    slope_on = remote(slopes.at[1], slopes.at[2], slope_send.at[2], slope_recv.at[2], core)
+    slope_side.start()
+    slope_core.start()
+    small_copies = [
+        remote(
+            small_ref.at[mate_quads[m]],
+            smalls.at[m - 1],
+            small_send.at[m - 1],
+            small_recv.at[m - 1],
+            mates[m],
+        )
+        for m in (1, 2, 3)
+    ]
+    for copy in small_copies:
+        copy.start()
+
+    squares[...] = jnp.zeros_like(squares)
+    per_block = BLOCK // ROWS
+    blocks = grad_chunks // per_block
+
+    def product(m, block):
+        columns = pl.ds(pl.multiple_of(block * BLOCK, BLOCK), BLOCK)
+        right = slope_ref[...] if m == 0 else slopes[m - 1]
+        return row_contract(rows_ref[m, :, columns], right).reshape(per_block, ROWS, width)
+
+    def block_chunks(block):
+        return pl.ds(block * per_block, per_block)
+
+    def first_term(block, carry):
+        prod[block_chunks(block)] = product(0, block)
+        return carry
+
+    def later_term(m):
+        def term(block, carry):
+            prod[block_chunks(block)] += product(m, block)
+            return carry
+
+        return term
+
+    lax.fori_loop(0, blocks, first_term, 0)
+    slope_core.wait_recv()
+    lax.fori_loop(0, blocks, later_term(1), 0)
+    slope_side.wait_recv()
+    slope_on.start()
+    lax.fori_loop(0, blocks, later_term(2), 0)
+    slope_on.wait_recv()
+
+    toward = jnp.where(middle, 1, 0)
+
+    def up_copy(i):
+        return remote(up.at[i], landed.at[toward, i], up_send.at[i], up_recv.at[toward, i], inward)
+
+    def landed_wait(slot, i):
+        remote(up.at[i], landed.at[slot, i], up_send.at[i], up_recv.at[slot, i], inward).wait_recv()
+
+    def down_copy(i):
+        return remote(
+            out_ref.at[quad, i], out_ref.at[quad, i], down_send.at[i], down_recv.at[i], outward
+        )
+
+    def down_arrival(i):
+        return remote(
+            out_ref.at[quad, i], out_ref.at[quad, i], down_send.at[i], down_recv.at[i], inward
+        )
+
+    def side_copy(i):
+        return remote(
+            out_ref.at[quad, i], out_ref.at[quad, i], side_send.at[i], side_recv.at[i], side
+        )
+
+    def core_copy(slot, i):
+        rows = out_ref.at[mate_quads[2 * slot], i]
+        return remote(rows, rows, core_send.at[slot, i], core_recv.at[slot, i], core)
+
+    def add_squares(which, i):
+        wide = out_ref[which, i].astype(jnp.float32)
+        squares[which] += jnp.sum((wide * wide).reshape(ROWS // 8, 8, width), axis=0)
+
+    def go_up(i):
+        @pl.when((i < grad_chunks) & (lax.rem(i, per_block) == 0))
+        def _():
+            block = i // per_block
+            prod[block_chunks(block)] += product(3, block)
+
+        @pl.when(i == grad_chunks)
+        def _():
+            total = small_ref[quad].astype(jnp.float32)
+            for m, copy in enumerate(small_copies):
+                copy.wait_recv()
+                total = total + smalls[m].astype(jnp.float32)
+            prod[grad_chunks] = total
+
+        @pl.when(depth > 0)
+        def _():
+            landed_wait(0, i)
+            up[i] = (prod[i] + landed[0, i].astype(jnp.float32)).astype(jnp.bfloat16)
+
+        @pl.when(depth == 0)
+        def _():
+            up[i] = prod[i].astype(jnp.bfloat16)
+
+        up_copy(i).start()
+
+    def go_down(i):
+        @pl.when(middle)
+        def _():
+            landed_wait(1, i)
+            out_ref[quad, i] = (
+                up[i].astype(jnp.float32) + landed[1, i].astype(jnp.float32)
+            ).astype(jnp.bfloat16)
+
+        @pl.when(jnp.logical_not(middle))
+        def _():
+            down_arrival(i).wait_recv()
+
+        @pl.when(depth > 0)
+        def _():
+            down_copy(i).start()
+
+        side_copy(i).start()
+        core_copy(0, i).start()
+        add_squares(quad, i)
+
+    def hand_on(i):
+        side_copy(i).wait_recv()
+        core_copy(1, i).start()
+        add_squares(mate_quads[2], i)
+
+    def take_in(i):
+        core_copy(0, i).wait_recv()
+        core_copy(1, i).wait_recv()
+        add_squares(mate_quads[1], i)
+        add_squares(mate_quads[3], i)
+
+    lag = 1 + 5 * (line // 2 - 1 - depth)
+    longest = 1 + 5 * (line // 2 - 1)
+
+    def step(t, carry):
+        for behind, action in ((0, go_up), (lag, go_down), (lag + 2, hand_on), (lag + 3, take_in)):
+            i = t - behind
+
+            @pl.when((i >= 0) & (i < chunks))
+            def _(i=i, action=action):
+                action(i)
+
+        return carry
+
+    lax.fori_loop(0, chunks + longest + 3, step, 0)
+
+    total = squares[0] + squares[1] + squares[2] + squares[3]
+    folded = total[:, :128]
+    for column in range(128, width, 128):
+        folded = folded + total[:, column : column + 128]
+    tp_squares[tp] = folded
+    tp_copies = [
+        remote(
+            tp_squares.at[tp],
+            tp_squares.at[tp],
+            tp_send.at[shift - 1],
+            tp_recv.at[shift - 1],
+            me,
+            lax.rem(tp + shift, n_tp),
+        )
+        for shift in range(1, n_tp)
+    ]
+    for copy in tp_copies:
+        copy.start()
+
+    def drain(i, carry):
+        up_copy(i).wait_send()
+
+        @pl.when(depth > 0)
+        def _():
+            down_copy(i).wait_send()
+
+        side_copy(i).wait_send()
+        core_copy(0, i).wait_send()
+        core_copy(1, i).wait_send()
+        return carry
+
+    lax.fori_loop(0, chunks, drain, 0)
+    for copy in [slope_side, slope_core, slope_on] + small_copies:
+        copy.wait_send()
+    for shift in range(1, n_tp):
+        source = lax.rem(tp + n_tp - shift, n_tp)
+        remote(
+            tp_squares.at[source],
+            tp_squares.at[source],
+            tp_send.at[shift - 1],
+            tp_recv.at[shift - 1],
+            me,
+            lax.rem(tp + shift, n_tp),
+        ).wait_recv()
+    for copy in tp_copies:
+        copy.wait_send()
+    everything = tp_squares[0]
+    for other in range(1, n_tp):
+        everything = everything + tp_squares[other]
+    everything = jnp.sum(jnp.sum(everything, axis=0, keepdims=True), axis=1, keepdims=True)
+    rescale_ref[...] = jnp.broadcast_to(
+        lax.rsqrt(everything / scale_count + 1e-06), rescale_ref.shape
+    )
+
+
+def grad_sums(mesh, rows, slope, small, scale_count):
+    n_ctx, n_tp = mesh.shape["ctx"], mesh.shape["tp"]
+    positions, width = slope.shape
+    chunks = rows.shape[2] // ROWS + 1
+    dma = pltpu.SemaphoreType.DMA
+    return pl.pallas_call(
+        functools.partial(grad_kernel, n_ctx, n_tp, float(scale_count)),
+        out_shape=(
+            jax.ShapeDtypeStruct((QUADS, chunks, ROWS, width), jnp.bfloat16),
+            jax.ShapeDtypeStruct((8, 128), jnp.float32),
+        ),
+        in_specs=[pl.BlockSpec(memory_space=pltpu.VMEM)] * 3,
+        out_specs=(pl.BlockSpec(memory_space=pltpu.VMEM),) * 2,
+        scratch_shapes=[
+            pltpu.VMEM((3, positions, width), jnp.bfloat16),
+            pltpu.VMEM((3, ROWS, width), jnp.bfloat16),
+            pltpu.VMEM((chunks, ROWS, width), jnp.float32),
+            pltpu.VMEM((chunks, ROWS, width), jnp.bfloat16),
+            pltpu.VMEM((2, chunks, ROWS, width), jnp.bfloat16),
+            pltpu.VMEM((QUADS, 8, width), jnp.float32),
+            pltpu.VMEM((n_tp, 8, 128), jnp.float32),
+            dma((3,)),
+            dma((3,)),
+            dma((3,)),
+            dma((3,)),
+            dma((chunks,)),
+            dma((2, chunks)),
+            dma((chunks,)),
+            dma((chunks,)),
+            dma((chunks,)),
+            dma((chunks,)),
+            dma((2, chunks)),
+            dma((2, chunks)),
+            dma((max(n_tp - 1, 1),)),
+            dma((max(n_tp - 1, 1),)),
+        ],
+        compiler_params=pltpu.CompilerParams(
+            collective_id=0, has_side_effects=True, vmem_limit_bytes=48 * 1024 * 1024
+        ),
+        cost_estimate=pl.CostEstimate(
+            flops=2 * QUADS * positions * rows.shape[2] * width,
+            bytes_accessed=4 * chunks * ROWS * width * 4,
+            transcendentals=0,
+        ),
+    )(rows, slope, small)
+
+
+def quarter_rows(mesh, gathered):
+    n_ctx = mesh.shape["ctx"]
+    quarter = gathered.shape[1] // QUADS
+    quad = lax.rem(lax.axis_index("ctx"), QUADS)
+    parts = []
+    for m in range(QUADS):
+        part = lax.dynamic_slice_in_dim(gathered, (quad ^ m) * quarter, quarter, 1)
+        if m:
+            part = lax.ppermute(part, "ctx", [(i, i ^ m) for i in range(n_ctx)])
+        parts.append(part)
+    return parts
 
 
 def on_device(
+    mesh,
     attended,
     out_proj,
     residual,
@@ -68,6 +411,7 @@
         hidden * lax.rsqrt(jnp.mean(hidden * hidden, axis=-1, keepdims=True) + 1e-05) * norm_gain
     ).astype(jnp.bfloat16)
     gathered = lax.all_gather(normed, "tp", axis=0, tiled=True)
+    near_rows = quarter_rows(mesh, gathered)
     condition = jnp.dot(gathered, cond_proj, preferred_element_type=jnp.float32)
     preact = condition[:, None, :] + jnp.einsum(
         "rsn,nh->rsh", noise_draws, noise_proj, preferred_element_type=jnp.float32
@@ -79,27 +423,32 @@
     own_samples = lax.psum_scatter(partial_samples, "tp", scatter_dimension=0, tiled=True)
     energies, own_slopes = energy_score(own_samples, targets.astype(jnp.float32))
     slopes = lax.all_gather(own_slopes, "tp", axis=0, tiled=True)
-    latent_part = jnp.einsum("rsh,rsl->hl", activation, slopes, preferred_element_type=jnp.float32)
+    latent_part = jnp.einsum("rsh,rsl->lh", activation, slopes, preferred_element_type=jnp.float32)
     backward = jnp.einsum("rsl,hl->rsh", slopes, latent_proj, preferred_element_type=jnp.float32)
     pre_grad = (backward * silu_slope(preact)).astype(jnp.bfloat16)
     noise_part = jnp.einsum(
         "rsn,rsh->nh", noise_draws, pre_grad, preferred_element_type=jnp.float32
     )
     cond_slope = jnp.sum(pre_grad, axis=1, dtype=jnp.float32).astype(jnp.bfloat16)
-    cond_part = row_contract(gathered, cond_slope)
-    param_count = D * HW + NZ * HW + HW * LAT
-    cond_sum, noise_sum, latent_sum = lax.psum((cond_part, noise_part, latent_part), "ctx")
-    squares_total = lax.psum(square_sum(cond_sum, noise_sum, latent_sum), "tp")
-    rescale = lax.rsqrt(squares_total / param_count + 1e-06)
-    cond_out = (cond_sum * rescale).astype(jnp.bfloat16)
-    noise_out = (noise_sum * rescale).astype(jnp.bfloat16)
-    latent_out = (latent_sum * rescale).astype(jnp.bfloat16)
-    return (energies, cond_out, noise_out, latent_out)
+    width = cond_slope.shape[1]
+    small = jnp.concatenate([noise_part, latent_part], axis=0).astype(jnp.bfloat16)
+    sums, rescale = grad_sums(
+        mesh,
+        jnp.stack(near_rows),
+        cond_slope,
+        small.reshape(QUADS, ROWS, width),
+        D * HW + NZ * HW + HW * LAT,
+    )
+    rescale = rescale[0, 0]
+    scaled = (sums.astype(jnp.float32) * rescale).astype(jnp.bfloat16)
+    cond_out = scaled[:, :-1].reshape(D, width)
+    small_out = scaled[:, -1].reshape(NZ + LAT, width)
+    return (energies, cond_out, small_out[:NZ], small_out[NZ:].T)
 
 
 def solution(mesh):
     return jax.shard_map(
-        on_device,
+        functools.partial(on_device, mesh),
         mesh=mesh,
         in_specs=(
             P("ctx", "tp"),

time: 519 us -> 280 us (0.54)
  waiting for transfers between devices: 404 us -> 91.1 us
  Pallas kernels: 0 us -> 88.9 us
  local copies, waits for them, and re-layouts: 5.77 us -> 19.2 us
  other arithmetic: 34.5 us -> 22.8 us
  matrix products: 43 us -> 32.7 us
    psum x1 -> x0, waiting for transfers between devices: 316 us -> none  [on_device(): lax.psum((cond_part, noise_part, latent_part), 'ctx')]
    pallas_call x0 -> x1, Pallas kernels: none -> 88.9 us  [grad_sums(): pl.pallas_call(functools.partial(grad_kernel, n_ctx, n_tp, float(scale_co...]
    ppermute x0 -> x3, waiting for transfers between devices: none -> 23.6 us  [quarter_rows(): part = lax.ppermute(part, 'ctx', [(i, i ^ m) for i in range(n_ctx)])]
    reduce_scatter x1, waiting for transfers between devices: 20.4 us -> 0.02 us  [on_device(): lax.psum_scatter(partial_samples, 'tp', scatter_dimension=0, tiled=True)]
    reduce_sum x3 -> x0, other arithmetic: 14.2 us -> none  [the longest x1 10.7 us: square_sum(): jnp.sum(cond_part * cond_part) + jnp.sum(noise_part * noise_part)]
    slice x0 -> x4, local copies, waits for them, and re-layouts: none -> 11.8 us  [the longest x1 8.67 us: on_device(): cond_out = scaled[:, :-1].reshape(D, width)]
    dot_general x2 -> x1, matrix products: 10.2 us -> 0.73 us  [on_device(): jnp.einsum('rsh,rsl->lh', activation, slopes, preferred_element_type=jnp....]
    psum x1 -> x0, blocking collectives: 5.42 us -> none  [on_device(): squares_total = lax.psum(square_sum(cond_sum, noise_sum, latent_sum), 'tp')]
  transfers between devices with their start and end apart: 4 -> 6, of which waited for: 4 -> 4; matrix products, arithmetic and copies ran while one was open for 0% -> 0% of each run, Pallas kernels for 0% -> 0%
where the time goes in v1:
time: 280 us
  waiting for transfers between devices  91.1 us (33%)
  Pallas kernels  88.9 us (32%)
  matrix products  32.7 us (12%)
  other arithmetic  22.8 us (8%)
  local copies, waits for them, and re-layouts  19.2 us (7%)
  between operations  14 us (5%)
  blocking collectives  9.16 us (3%)
    pallas_call x1, Pallas kernels, grad_sums(): pl.pallas_call(functools.partial(grad_kernel, n_ctx, n_tp, float(scale_co...  88.9 us
    reduce_scatter x1, waiting for transfers between devices, on_device(): lax.psum_scatter(jnp.dot(attended, out_proj, preferred_element_type=jnp.f...  34.6 us
    all_gather x1, waiting for transfers between devices, on_device(): gathered = lax.all_gather(normed, 'tp', axis=0, tiled=True)  32.9 us
    ppermute x3, waiting for transfers between devices, quarter_rows(): part = lax.ppermute(part, 'ctx', [(i, i ^ m) for i in range(n_ctx)])  23.6 us
    dot_general x1, matrix products, on_device(): jnp.dot(attended, out_proj, preferred_element_type=jnp.float32)  11.4 us
    convert_element_type x1, other arithmetic, on_device(): scaled = (sums.astype(jnp.float32) * rescale).astype(jnp.bfloat16)  10.9 us
    all_gather x1, blocking collectives, on_device(): slopes = lax.all_gather(own_slopes, 'tp', axis=0, tiled=True)  9.16 us
    slice x1, local copies, waits for them, and re-layouts, on_device(): cond_out = scaled[:, :-1].reshape(D, width)  8.67 us
  transfers between devices with their start and end apart: 6, of which 4 were waited for; matrix products, arithmetic and copies ran while one was open for 0% of the time, Pallas kernels for 0%

profile of v1, /device:TPU:0, one launch (start us, length us, event | category | flops | bytes accessed | tf_op | source)
XLA Modules:
  0.0 280.0 jit_solution(1392760281688583872)
XLA Ops:
  7.2 1.2 copy-done
  8.4 11.4 %convolution_convert_fusion = bf16[256,4096]{1,0:T(8,128)(2,1)} fusion(bf16[256,2048]{1,0:T(8,128)(2,1)S(1)} %copy-done, bf16[2048,4096]{1,0:T(8,128)(2,1)} %param.10), kind=kOutput, calls=%fused_computation.6 | convolution fusion | flops 4296015872 | bytes 19922944 | tf_op jit(solution)/shard_map/dot_general | solution.py:404
  19.9 34.6 %reduce-scatter.3.cloned.1.call-done = bf16[128,4096]{1,0:T(8,128)(2,1)} async-done(((bf16[256,4096]{1,0:T(8,128)(2,1)}), bf16[128,4096]{1,0:T(8,128)(2,1)}) %reduce-scatter.3.cloned.1.call-update) | async-done | bytes 1048592 | tf_op jit(solution)/shard_map/reduce_scatter | solution.py:403
  54.5 1.6 multiply_reduce_fusion
  56.2 2.6 multiply_convert_fusion.3
  59.2 32.9 %all-gather.2.cloned.1.call-done = bf16[256,4096]{1,0:T(8,128)(2,1)} async-done(((bf16[128,4096]{1,0:T(8,128)(2,1)}), bf16[256,4096]{1,0:T(8,128)(2,1)}) %all-gather.2.cloned.1.call-update) | async-done | bytes 2097168 | tf_op jit(solution)/shard_map/all_gather | solution.py:413
  92.1 6.3 %fusion.16 = f32[256,1024]{1,0:T(8,128)S(1)} fusion(bf16[256,4096]{1,0:T(8,128)(2,1)} %all-gather.2.cloned.1.call-done, bf16[4096,1024]{1,0:T(8,128)(2,1)} %param.13), kind=kOutput, calls=%fused_computation.43 | convolution fusion | flops 2147483648 | bytes 11534336 | tf_op jit(solution)/shard_map/dot_general | solution.py:415
  98.5 4.8 %multiply_convert_fusion.2 = (bf16[256,8,1024]{2,0,1:T(8,128)(2,1)S(1)}, f32[256,8,1024]{2,0,1:T(8,128)}) fusion(f32[256,1024]{1,0:T(8,128)S(1)} %fusion.16, bf16[256,8,128]{0,2,1:T(8,128)(2,1)S(1)} %copy.33, bf16[128,1024]{1,0:T(8,128)(2,1)S(1)} %copy-done.13), kind=kOutput, calls=%fused_computation.2 | convolution fusion | flops 549453824 | bytes 14417920 | tf_op jit(solution)/shard_map/rsn,nh->rsh/dot_general | solution.py:416
  103.3 2.1 copy-done.2
  105.4 2.3 fusion.8
  110.0 12.3 %collective-permute-done.2 = bf16[256,1024]{1,0:T(8,128)(2,1)S(1)} collective-permute-done((bf16[256,1024]{1,0:T(8,128)(2,1)S(1)}, bf16[256,1024]{1,0:T(8,128)(2,1)S(1)}, u32[]{:S(2)}, u32[]{:S(2)}) %collective-permute-start.2) | collective-permute-done | bytes 524320 | tf_op jit(solution)/shard_map/ppermute | solution.py:386
  122.3 11.3 %collective-permute-done.1 = bf16[256,1024]{1,0:T(8,128)(2,1)S(1)} collective-permute-done((bf16[256,1024]{1,0:T(8,128)(2,1)S(1)}, bf16[256,1024]{1,0:T(8,128)(2,1)S(1)}, u32[]{:S(2)}, u32[]{:S(2)}) %collective-permute-start.1) | collective-permute-done | bytes 524320 | tf_op jit(solution)/shard_map/ppermute | solution.py:386
  133.9 1.3 multiply_reduce_fusion.1
  135.2 1.4 copy.28
  136.6 1.9 fusion.1
  138.5 1.2 copy.30
  139.8 1.0 copy.31
  140.8 3.3 %fusion = f32[128,8,128]{2,1,0:T(8,128)S(1)} fusion(f32[128,8,8]{2,1,0:T(8,128)} %copy.31, f32[128,8,128]{2,1,0:T(8,128)S(1)} %copy.28), kind=kLoop, calls=%fused_computation.7 | loop fusion | flops 3014656 | bytes 1081344 | tf_op jit(solution)/shard_map/reduce_sum | solution.py:39
  144.3 9.2 %all_gather.7 = bf16[256,8,128]{2,0,1:T(8,128)(2,1)S(1)} all-gather(bf16[128,8,128]{2,0,1:T(8,128)(2,1)S(1)} %fusion.6), channel_id=1, replica_groups=mesh['ctx'=16,'tp'=2] {'tp'}, dimensions={0}, use_global_device_ids=true | all-gather | bytes 786432 | tf_op jit(solution)/shard_map/all_gather | solution.py:425
  154.2 6.4 %fusion.15 = (bf16[256,1024]{1,0:T(8,128)(2,1)S(1)}, bf16[256,8,1024]{2,0,1:T(8,128)(2,1)S(1)}) fusion(f32[256,8,1024]{2,0,1:T(8,128)} %get-tuple-element.19, f32[256,1024]{1,0:T(8,128)S(1)} %copy-done.15, bf16[256,8,128]{2,0,1:T(8,128)(2,1)S(1)} %all_gather.7, bf16[1024,128]{1,0:T(8,128)(2,1)S(1)} %copy-done.10), kind=kOutput, calls=%fused_computation.42 | convolution fusion | flops 559677440 | bytes 14942208 | tf_op jit(solution)/shard_map/rsl,hl->rsh/dot_general | solution.py:427
  161.4 88.9 %shard_map.120 = (bf16[4,17,64,1024]{3,2,1,0:T(8,128)(2,1)}, f32[8,128]{1,0:T(8,128)S(1)}) custom-call(bf16[4,256,1024]{2,1,0:T(8,128)(2,1)S(1)} %pad_maximum_fusion.rows_ref, bf16[256,1024]{1,0:T(8,128)(2,1)S(1)} %get-tuple-element.20.slope_ref, bf16[4,64,1024]{2,1,0:T(8,128)(2,1)S(1)} %bitcast.46), custom_call_target="tpu_custom_call" | custom-call | flops 2147483648 | bytes 17825792 | tf_op jit(solution)/shard_map/pallas_call | solution.py:336
  250.8 10.9 %multiply_convert_fusion = bf16[4,17,64,1024]{3,2,1,0:T(8,128)(2,1)} fusion(bf16[4,17,64,1024]{3,2,1,0:T(8,128)(2,1)} %get-tuple-element.6, f32[]{:T(128)} %bitcast.10), kind=kLoop, calls=%fused_computation | loop fusion | flops 13369344 | bytes 17825796 | tf_op jit(solution)/shard_map/convert_element_type | solution.py:443
  261.7 1.8 fusion.14
  263.5 8.7 %slice.27 = bf16[4,16,64,1024]{3,2,1,0:T(8,128)(2,1)} slice(bf16[4,17,64,1024]{3,2,1,0:T(8,128)(2,1)} %multiply_convert_fusion), slice={[0:4], [0:16], [0:64], [0:1024]} | slice | bytes 16777216 | tf_op jit(solution)/shard_map/slice | solution.py:444
  (56 shorter events, 6.8 us)
Async XLA Ops:
  7.2 1.2 copy-start
  7.2 47.3 %copy-start.5 = (bf16[128,4096]{1,0:T(8,128)(2,1)S(1)}, bf16[128,4096]{1,0:T(8,128)(2,1)}, u32[]{:S(2)}) copy-start(bf16[128,4096]{1,0:T(8,128)(2,1)} %param.11) | copy-start | bytes 3145732
  7.2 47.3 %reduce-scatter.3.cloned.1.call-start = ((), (), s32[]{:S(2)}) async-start(), calls=%async_computation.2 | async-start | bytes 3145728 | tf_op jit(solution)/shard_map/reduce_scatter | solution.py:403
  19.8 36.3 %copy-start.12 = (f32[4096]{0:T(1024)S(1)}, f32[4096]{0:T(1024)}, u32[]{:S(2)}) copy-start(f32[4096]{0:T(1024)} %param.12) | copy-start | bytes 49156
  19.8 39.0 %copy-start.9 = (bf16[256,8,128]{2,1,0:T(8,128)(2,1)S(1)}, bf16[256,8,128]{2,1,0:T(8,128)(2,1)}, u32[]{:S(2)}) copy-start(bf16[256,8,128]{2,1,0:T(8,128)(2,1)} %param.16) | copy-start | bytes 1572868
  19.9 72.2 %all-gather.2.cloned.1.call-start = ((), (), s32[]{:S(2)}) async-start(), calls=%async_computation.3 | async-start | bytes 3145728 | tf_op jit(solution)/shard_map/all_gather | solution.py:413
  58.8 75.0 %reduce-scatter.5.cloned.1.call-start = ((), (), s32[]{:S(2)}) async-start(), calls=%async_computation.4 | async-start | bytes 1572864 | tf_op jit(solution)/shard_map/reduce_scatter | solution.py:423
  59.2 39.2 %copy-start.6 = (bf16[256,8,128]{0,2,1:T(8,128)(2,1)}, bf16[256,8,128]{0,2,1:T(8,128)(2,1)S(1)}, u32[]{:S(2)}) copy-start(bf16[256,8,128]{0,2,1:T(8,128)(2,1)S(1)} %copy.33) | copy-start | bytes 1572868
  59.2 39.2 %copy-start.13 = (bf16[128,1024]{1,0:T(8,128)(2,1)S(1)}, bf16[128,1024]{1,0:T(8,128)(2,1)}, u32[]{:S(2)}) copy-start(bf16[128,1024]{1,0:T(8,128)(2,1)} %param.14) | copy-start | bytes 786436
  98.5 4.8 %copy-start.14 = (f32[256,1024]{1,0:T(8,128)}, f32[256,1024]{1,0:T(8,128)S(1)}, u32[]{:S(2)}) copy-start(f32[256,1024]{1,0:T(8,128)S(1)} %fusion.16) | copy-start | bytes 3145732
  98.5 7.0 %copy-start.10 = (bf16[1024,128]{1,0:T(8,128)(2,1)S(1)}, bf16[1024,128]{1,0:T(8,128)(2,1)}, u32[]{:S(2)}) copy-start(bf16[1024,128]{1,0:T(8,128)(2,1)} %param.15) | copy-start | bytes 786436
  103.3 2.1 copy-start.2
  103.3 4.5 %copy-start.8 = (bf16[256,4096]{1,0:T(8,128)(2,1)S(1)}, bf16[256,4096]{1,0:T(8,128)(2,1)}, u32[]{:S(2)}) copy-start(bf16[256,4096]{1,0:T(8,128)(2,1)} %all-gather.2.cloned.1.call-done) | copy-start | bytes 6291460
  105.4 4.5 %copy-start.11 = (bf16[128,128]{1,0:T(8,128)(2,1)S(1)}, bf16[128,128]{1,0:T(8,128)(2,1)}, u32[]{:S(2)}) copy-start(bf16[128,128]{1,0:T(8,128)(2,1)} %param.17) | copy-start | bytes 98308
  108.0 14.3 %collective-permute-start.2 = (bf16[256,1024]{1,0:T(8,128)(2,1)S(1)}, bf16[256,1024]{1,0:T(8,128)(2,1)S(1)}, u32[]{:S(2)}, u32[]{:S(2)}) collective-permute-start(bf16[256,1024]{1,0:T(8,128)(2,1)S(1)} %get-tuple-element.11), channel_id=1, source_target_pairs={{0,6},{2,4},{4,2},{6,0},{8,14},{10,12},{12,10},{14,8},{16,22},{18,... | collective-permute-start | bytes 1572872 | tf_op jit(solution)/shard_map/ppermute | solution.py:386
  109.0 24.5 %collective-permute-start.1 = (bf16[256,1024]{1,0:T(8,128)(2,1)S(1)}, bf16[256,1024]{1,0:T(8,128)(2,1)S(1)}, u32[]{:S(2)}, u32[]{:S(2)}) collective-permute-start(bf16[256,1024]{1,0:T(8,128)(2,1)S(1)} %get-tuple-element.12), channel_id=1, source_target_pairs={{0,4},{2,6},{4,0},{6,2},{8,12},{10,14},{12,8},{14,10},{16,20},{18,... | collective-permute-start | bytes 1572872 | tf_op jit(solution)/shard_map/ppermute | solution.py:386
  109.6 23.9 %collective-permute-start = (bf16[256,1024]{1,0:T(8,128)(2,1)S(1)}, bf16[256,1024]{1,0:T(8,128)(2,1)S(1)}, u32[]{:S(2)}, u32[]{:S(2)}) collective-permute-start(bf16[256,1024]{1,0:T(8,128)(2,1)S(1)} %get-tuple-element.13), channel_id=1, source_target_pairs={{0,2},{2,0},{4,6},{6,4},{8,10},{10,8},{12,14},{14,12},{16,18},{18,... | collective-permute-start | bytes 1572872 | tf_op jit(solution)/shard_map/ppermute | solution.py:386
  133.8 10.2 %copy-start.4 = (f32[128,8,128]{2,0,1:T(8,128)S(1)}, f32[128,8,128]{2,0,1:T(8,128)}, u32[]{:S(2)}) copy-start(f32[128,8,128]{2,0,1:T(8,128)} %reduce-scatter.5.cloned.1.call-done) | copy-start | bytes 1572868
  140.8 12.7 %copy-start.3 = (bf16[256,8,1024]{2,0,1:T(8,128)(2,1)S(1)}, bf16[256,8,1024]{2,0,1:T(8,128)(2,1)}, u32[]{:S(2)}) copy-start(bf16[256,8,1024]{2,0,1:T(8,128)(2,1)} %copy-done.2) | copy-start | bytes 12582916
  140.8 13.4 %copy-start.15 = (f32[256,1024]{1,0:T(8,128)S(1)}, f32[256,1024]{1,0:T(8,128)}, u32[]{:S(2)}) copy-start(f32[256,1024]{1,0:T(8,128)} %copy-done.14) | copy-start | bytes 3145732
  154.2 6.4 %copy-start.7 = (bf16[256,8,128]{0,2,1:T(8,128)(2,1)S(1)}, bf16[256,8,128]{0,2,1:T(8,128)(2,1)}, u32[]{:S(2)}) copy-start(bf16[256,8,128]{0,2,1:T(8,128)(2,1)} %copy-done.6) | copy-start | bytes 1572868
  263.5 10.0 %copy-start.1 = (bf16[256,2048]{1,0:T(8,128)(2,1)S(1)}, bf16[256,2048]{1,0:T(8,128)(2,1)}, u32[]{:S(2)}) copy-start(bf16[256,2048]{1,0:T(8,128)(2,1)} %param.9) | copy-start | bytes 3145732
Sparse Core Ops, SparseCore 0:
  20.0 34.4 reduce-scatter.2
  58.9 33.1 all-gather.1
  107.9 20.3 reduce-scatter.4
